TPU v7x, 256 devices: a whole 4x4x8 slice. The times are simulated.
256 devices in a mesh: prow: 32 (over z_hi, x, core), pcol: 8 (over z_lo, y).
Axes of the slice: x: 4, y: 4, z: 8 (z_hi: 4, z_lo: 2; z = z_hi * 2 + z_lo), core: 2. Of those that a mesh axis runs over, the one named last changes fastest.
Arguments:
- matrix: float32 [40960, 8192], P('prow', 'pcol'), may hold values from -6 to 6
- pivots: int32 [2, 256], replicated, may hold values from 0 to 40959, as said below
- lower_inverse: float32 [2, 256, 256], replicated, as said below
- upper_inverse: float32 [2, 256, 256], replicated, as said below
Outputs:
- factored: float32 [40960, 8192], P('prow', 'pcol')
Inputs may be any that keep to these rules, and one draw needn't show every extreme that they name: `pivots`: the 512 pivot indices are distinct over both steps and none lies in rows k * 1280 to k * 1280 + 255 for k = 0 or 1. `lower_inverse`: unit lower triangular. `upper_inverse`: upper triangular with positive diagonal.
All inputs are finite; a program needn't handle non-finite values.
Results may differ from a plain program's by a relative error of at most 0.0001.
Values sent between devices are 32-bit elements; how exact they have to be, the bound alone decides.
No kernel may reach another device: no remote copies, remote signals or barrier semaphores. Data moves between devices by JAX's collectives and lax.ppermute only.
A program may use at most 64 MiB of HBM per device.

v0:
```python
import functools

import jax
import jax.numpy as jnp
from jax import lax
from jax.experimental import pallas as pl
from jax.experimental.pallas import tpu as pltpu
from jax.sharding import PartitionSpec as P

NB = 256
ROWS_DEV = 1280
COLS_DEV = 1024
XS = 4
ZS = 4
QUARTER = NB // XS
SUB = QUARTER // ZS
BLOCK = 640
SMALL_BLOCK = 320
PART = ROWS_DEV // 8
HALF = 32


def shift(core, x, z):
    pairs = []
    for index in range(2 * XS * ZS):
        c, xi, zi = index % 2, index // 2 % XS, index // (2 * XS)
        target = ((zi + z) % ZS * XS + (xi + x) % XS) * 2 + (c + core) % 2
        pairs.append((index, target))
    return pairs


def send(value, core=0, x=0, z=0):
    return lax.ppermute(value, "prow", shift(core, x, z))


def send_from(value, keep, core=0, x=0, z=0):
    pairs = [pair for pair in shift(core, x, z) if keep(pair[0] // 2 % XS, pair[0] // (2 * XS))]
    return lax.ppermute(value, "prow", pairs)


def owned_rows(pivots, prow, number):
    local = pivots.reshape(2 * NB) - prow * ROWS_DEV
    owned = (local >= 0) & (local < ROWS_DEV)
    index = lax.broadcasted_iota(jnp.int32, (2 * NB, 2 * NB), 0)
    other = lax.broadcasted_iota(jnp.int32, (2 * NB, 2 * NB), 1)
    before = jnp.sum(jnp.where(owned[None, :] & (other < index), 1, 0), axis=1)
    slot = jnp.where(owned, before, 2 * NB)
    packed = local * (2 * NB) + number
    entries = jnp.sum(jnp.where(slot[None, :] == index, packed[None, :], 0), axis=1)
    return entries, jnp.sum(jnp.where(owned, 1, 0)).reshape(1)


def pick_kernel(place, entries, count, a_ref, mine, theirs, panel, top, sem, panel_sem, top_sem):
    x, z, core = place[1], place[2], place[3]
    copies = [
        pltpu.make_async_copy(
            a_ref.at[(n % 4 * 2 + n // 4) * PART:(n % 4 * 2 + n // 4 + 1) * PART, :NB],
            panel.at[n * PART:(n + 1) * PART, :],
            panel_sem.at[n],
        )
        for n in range(8)
    ]
    copies.append(pltpu.make_async_copy(a_ref.at[:NB, :], top, top_sem))
    for copy in copies:
        copy.start()
    mine[...] = jnp.zeros_like(mine)
    theirs[...] = jnp.zeros_like(theirs)

    def start(n, carry):
        local, number = entries[n] // (2 * NB), entries[n] % (2 * NB)
        i = number % NB
        quarter, sub, low = i // QUARTER, i // SUB % ZS, i % SUB
        dest = (quarter - x + XS) % XS * QUARTER + (sub - z + ZS) % ZS * SUB + low
        own = core == number // NB
        row = a_ref.at[pl.ds(local, 1), :]

        @pl.when(own)
        def _():
            pltpu.make_async_copy(row, mine.at[pl.ds(dest, 1), :], sem).start()

        @pl.when(jnp.logical_not(own))
        def _():
            pltpu.make_async_copy(row, theirs.at[pl.ds(dest, 1), :], sem).start()

        return carry

    def wait(n, carry):
        pltpu.make_async_copy(a_ref.at[pl.ds(0, 1), :], mine.at[pl.ds(0, 1), :], sem).wait()
        return carry

    lax.fori_loop(0, count[0], start, 0)
    lax.fori_loop(0, count[0], wait, 0)
    for copy in copies:
        copy.wait()


def pick(place, entries, count, matrix):
    smem = pl.BlockSpec(memory_space=pltpu.SMEM)
    vmem = pl.BlockSpec(memory_space=pltpu.VMEM)
    half = jax.ShapeDtypeStruct((NB, COLS_DEV), jnp.float32)
    return pl.pallas_call(
        pick_kernel,
        out_shape=[half, half, jax.ShapeDtypeStruct((ROWS_DEV, NB), jnp.float32), half],
        in_specs=[smem, smem, smem, pl.BlockSpec(memory_space=pltpu.HBM)],
        out_specs=[vmem] * 4,
        scratch_shapes=[
            pltpu.SemaphoreType.DMA, pltpu.SemaphoreType.DMA((8,)), pltpu.SemaphoreType.DMA
        ],
        compiler_params=pltpu.CompilerParams(vmem_limit_bytes=8 * 1024 * 1024),
        name="pick_rows",
    )(place, entries, count, matrix)


def split(value):
    high = value.astype(jnp.bfloat16)
    low = (value - high.astype(jnp.float32)).astype(jnp.bfloat16)
    return high, low


def mul(a, b):
    left = jnp.concatenate([a[0], a[1], a[0]], axis=1)
    right = jnp.concatenate([b[1], b[0], b[0]], axis=0)
    return jnp.dot(left, right, preferred_element_type=jnp.float32)


def three(value):
    high, rest = value.astype(jnp.bfloat16), None
    rest = value - high.astype(jnp.float32)
    middle = rest.astype(jnp.bfloat16)
    return high, middle, (rest - middle.astype(jnp.float32)).astype(jnp.bfloat16)


def spread_kernel(place, own_ref, other_ref, pick_own, pick_other, *refs):
    outs = refs[-XS:]

    @pl.when((place[1] == 0) & (place[2] == 0))
    def _():
        rows = ZS * HALF
        for n in range(COLS_DEV // NB):
            cols = slice(n * NB, (n + 1) * NB)
            own, other = three(own_ref[:, cols]), three(other_ref[:, cols])
            for j in range(XS):
                block = slice(j * rows, (j + 1) * rows)
                dot = functools.partial(jnp.dot, preferred_element_type=jnp.float32)
                total = [
                    dot(pick_own[block, :], a) + dot(pick_other[block, :], b)
                    for a, b in zip(own, other)
                ]
                outs[j][:, cols] = total[0] + (total[1] + total[2])


def spread(place, own, other, picks, tokens):
    smem, vmem = pl.BlockSpec(memory_space=pltpu.SMEM), pl.BlockSpec(memory_space=pltpu.VMEM)
    anywhere = pl.BlockSpec(memory_space=pl.ANY)
    shape = jax.ShapeDtypeStruct((ZS * HALF, COLS_DEV), jnp.float32)
    return pl.pallas_call(
        spread_kernel,
        out_shape=[shape] * XS,
        in_specs=[smem, vmem, vmem, vmem, vmem] + [anywhere] * len(tokens),
        out_specs=[vmem] * XS,
        compiler_params=pltpu.CompilerParams(vmem_limit_bytes=16 * 1024 * 1024),
        name="spread_rows",
    )(place, own, other, *picks, *tokens)


def choose_kernel(axis, tokens, place, *refs):
    pieces, outs = refs[:4], refs[4 + tokens:]
    rows = outs[0].shape[0]
    for n, piece in enumerate(pieces):

        @pl.when(place[axis] == n)
        def _():
            for i, out in enumerate(outs):
                out[...] = piece[i * rows:(i + 1) * rows, :]


def choose(place, axis, pieces, count, tokens):
    smem, vmem = pl.BlockSpec(memory_space=pltpu.SMEM), pl.BlockSpec(memory_space=pltpu.VMEM)
    anywhere = pl.BlockSpec(memory_space=pl.ANY)
    rows, cols = pieces[0].shape
    return pl.pallas_call(
        functools.partial(choose_kernel, axis, len(tokens)),
        out_shape=[jax.ShapeDtypeStruct((rows // count, cols), jnp.float32)] * count,
        in_specs=[smem] + [vmem] * 4 + [anywhere] * len(tokens),
        out_specs=[vmem] * count,
        compiler_params=pltpu.CompilerParams(vmem_limit_bytes=8 * 1024 * 1024),
        name="choose_piece",
    )(place, *pieces, *tokens)


def update_kernel(
    packed, place, entries, count, a_ref, near_ref, far_ref, m_ref, w_ref, *refs
):
    pieces, displaced = refs[:2 * XS], refs[2 * XS:-10]
    out_ref, xs, uh, ul, top, ph, wh, wl, ch, cl = refs[-10:]
    prow, x, z, core, pcol = place[0], place[1], place[2], place[3], place[4]
    block, rows_block = pl.program_id(0), BLOCK if packed else SMALL_BLOCK

    @pl.when(block == 0)
    def _():
        for piece in range(2 * XS):
            step = core if piece < XS else 1 - core
            for k in range(ZS):
                dest = step * NB + (x - piece + 2 * XS) % XS * QUARTER + (z - k + ZS) % ZS * SUB
                dest = pl.multiple_of(dest, SUB)
                xs[pl.ds(dest, SUB), :] = pieces[piece][k * SUB:(k + 1) * SUB, :]
        w0, w1 = split(w_ref[0]), split(w_ref[1])
        wh[0], wl[0] = w0
        wh[1], wl[1] = w1
        m0, m1 = split(m_ref[0]), split(m_ref[1])
        l0r1 = mul(split(xs[NB:, COLS_DEV:]), w0)
        u0c1 = mul(m0, split(xs[:NB, COLS_DEV:]))
        ch[...], cl[...] = split(u0c1)
        l0r1s = split(l0r1)

        def upper(n, carry):
            cols = pl.ds(pl.multiple_of(n * width, width), width)
            u0 = mul(m0, split(xs[:NB, cols]))
            u0s = split(u0)
            uh[:NB, cols], ul[:NB, cols] = u0s
            y1 = xs[NB:, cols] - mul(l0r1s, u0s)
            u1 = mul(m1, split(y1))
            uh[NB:, cols], ul[NB:, cols] = split(u1)

            @pl.when(prow == 0)
            def _():
                top[:, cols] = u0

            @pl.when(prow == 1)
            def _():
                top[:, cols] = u1

                @pl.when((pcol == 1) & (n == 0))
                def _():
                    top[:, :NB] = y1[:, :NB]

            return carry

        width = COLS_DEV if packed else NB
        lax.fori_loop(0, COLS_DEV // width, upper, 0)

        @pl.when((prow == 0) & (pcol == 0))
        def _():
            top[:, :NB] = xs[:NB, :NB]

        @pl.when((prow == 1) & (pcol == 0))
        def _():
            top[:, :NB] = l0r1

    out_ref[...] = a_ref[...]
    for y in range(rows_block // (2 * PART)):
        rows = slice(y * PART, (y + 1) * PART)
        first, second = slice(2 * y * PART, (2 * y + 1) * PART), slice((2 * y + 1) * PART, (2 * y + 2) * PART)

        @pl.when(pcol < 4)
        def _():
            ph[first, :] = near_ref[rows, :]
            ph[second, :] = far_ref[rows, :]

        @pl.when(pcol >= 4)
        def _():
            ph[first, :] = far_ref[rows, :]
            ph[second, :] = near_ref[rows, :]

    base = block * rows_block

    def patch(n, carry):
        local, number = entries[n] // (2 * NB) - base, entries[n] % (2 * NB)

        @pl.when((local >= 0) & (local < rows_block))
        def _():
            if packed:
                src = number % HALF
                piece = jnp.where(core == number // HALF, 0, 1)
            else:
                i = number % NB
                src = (z - i // SUB % ZS + ZS) % ZS * SUB + i % SUB
                piece = jnp.where(core == number // NB, 0, XS) + (x - i // QUARTER + XS) % XS
            for j in range(len(displaced)):

                @pl.when(piece == j)
                def _():
                    row = displaced[j][pl.ds(src, 1), :]
                    out_ref[pl.ds(local, 1), :] = row[:, :COLS_DEV]
                    ph[pl.ds(local, 1), :] = row[:, COLS_DEV:]

        return carry

    lax.fori_loop(0, count[0], patch, 0)
    l0 = mul(split(ph[:, :NB]), (wh[0], wl[0]))
    l0s = split(l0)
    l1 = mul(split(ph[:, NB:] - mul(l0s, (ch[...], cl[...]))), (wh[1], wl[1]))
    ls = tuple(jnp.concatenate([a, b], axis=1) for a, b in zip(l0s, split(l1)))

    def subtract(n, carry):
        cols = pl.ds(pl.multiple_of(n * NB, NB), NB)
        out_ref[:, cols] = out_ref[:, cols] - mul(ls, (uh[:, cols], ul[:, cols]))
        return carry

    lax.fori_loop(0, COLS_DEV // NB, subtract, 0, unroll=packed)

    @pl.when(pcol == 0)
    def _():
        out_ref[:, :NB] = l0

    @pl.when(pcol == 1)
    def _():
        out_ref[:, :NB] = l1

    @pl.when((block == 0) & (prow < 2))
    def _():
        out_ref[:NB, :] = top[...]


def update(packed, place, entries, count, matrix, near, far, lower, upper, pieces, displaced):
    smem = pl.BlockSpec(memory_space=pltpu.SMEM)
    vmem = pl.BlockSpec(memory_space=pltpu.VMEM)
    f32, bf16 = jnp.float32, jnp.bfloat16
    rows_block = BLOCK if packed else SMALL_BLOCK
    wide = pl.BlockSpec((rows_block, COLS_DEV), lambda i: (i, 0))
    half = pl.BlockSpec((rows_block // 2, 2 * NB), lambda i: (i, 0))
    return pl.pallas_call(
        functools.partial(update_kernel, packed),
        grid=(ROWS_DEV // rows_block,),
        out_shape=jax.ShapeDtypeStruct((ROWS_DEV, COLS_DEV), f32),
        in_specs=[smem, smem, smem, wide, half, half]
        + [vmem] * (2 + len(pieces) + len(displaced)),
        out_specs=wide,
        scratch_shapes=[
            pltpu.VMEM((2 * NB, COLS_DEV + NB), f32),
            pltpu.VMEM((2 * NB, COLS_DEV), bf16),
            pltpu.VMEM((2 * NB, COLS_DEV), bf16),
            pltpu.VMEM((NB, COLS_DEV), f32),
            pltpu.VMEM((rows_block, 2 * NB), f32),
            pltpu.VMEM((2, NB, NB), bf16),
            pltpu.VMEM((2, NB, NB), bf16),
            pltpu.VMEM((NB, NB), bf16),
            pltpu.VMEM((NB, NB), bf16),
        ],
        compiler_params=pltpu.CompilerParams(vmem_limit_bytes=40 * 1024 * 1024),
        name="panel_update",
    )(place, entries, count, matrix, near, far, lower, upper, *pieces, *displaced)


def add_kernel(n, tokens, *refs):
    parts, outs = refs[:n], refs[n + tokens:]
    rows = outs[0].shape[0]
    for i, out in enumerate(outs):
        block = slice(i * rows, (i + 1) * rows)
        value = parts[0][block, :]
        for part in parts[1:]:
            value = value + part[block, :]
        out[...] = value


def add(parts, count, tokens=()):
    vmem, anywhere = pl.BlockSpec(memory_space=pltpu.VMEM), pl.BlockSpec(memory_space=pl.ANY)
    rows, cols = parts[0].shape
    return pl.pallas_call(
        functools.partial(add_kernel, len(parts), len(tokens)),
        out_shape=[jax.ShapeDtypeStruct((rows // count, cols), jnp.float32)] * count,
        in_specs=[vmem] * len(parts) + [anywhere] * len(tokens),
        out_specs=[vmem] * count,
        compiler_params=pltpu.CompilerParams(vmem_limit_bytes=8 * 1024 * 1024),
        name="add_parts",
    )(*parts, *tokens)


def sync(*values):
    anywhere = pl.BlockSpec(memory_space=pl.ANY)
    return pl.pallas_call(
        lambda *refs: None,
        out_shape=[jax.ShapeDtypeStruct(value.shape, value.dtype) for value in values],
        in_specs=[anywhere] * len(values),
        out_specs=[anywhere] * len(values),
        input_output_aliases={i: i for i in range(len(values))},
        compiler_params=pltpu.CompilerParams(vmem_limit_bytes=1024 * 1024),
        name="sync",
    )(*values)


def pack_kernel(groups, count, *refs):
    parts, out = refs[:groups * count], refs[-1]
    col = 0
    for i in range(groups):
        rows, width = parts[i * count].shape
        for k in range(count):
            out[k * rows:(k + 1) * rows, col:col + width] = parts[i * count + k][...]
        col += width


def pack(groups, tokens=()):
    vmem, anywhere = pl.BlockSpec(memory_space=pltpu.VMEM), pl.BlockSpec(memory_space=pl.ANY)
    cols = sum(group[0].shape[1] for group in groups)
    parts = [part for group in groups for part in group]
    return pl.pallas_call(
        functools.partial(pack_kernel, len(groups), len(groups[0])),
        out_shape=jax.ShapeDtypeStruct((groups[0][0].shape[0] * len(groups[0]), cols), jnp.float32),
        in_specs=[vmem] * len(parts) + [anywhere] * len(tokens),
        out_specs=vmem,
        compiler_params=pltpu.CompilerParams(vmem_limit_bytes=8 * 1024 * 1024),
        name="pack_blocks",
    )(*parts, *tokens)


def gather_z(held):
    return [held] + [send(held, z=k) for k in range(1, ZS)]


def gather_x(held):
    pieces = [held] + [send(held, x=j) for j in range(1, XS)]
    return pieces + [send(piece, core=1) for piece in pieces]


def to_columns(value):
    rows = value.shape[0]
    value = lax.all_to_all(jnp.tile(value, (8, 1)), "pcol", 0, 0, tiled=True)
    return value[:rows], value[rows:2 * rows]


def panel_parts(panel):
    parts = lax.all_to_all(panel, "pcol", 0, 0, tiled=True)
    return jnp.concatenate([parts[:PART], parts[PART:2 * PART]], axis=1)


def along_y(parts):
    groups = [[0, 1, 2, 3], [4, 5, 6, 7]]
    return lax.all_to_all(
        jnp.tile(parts, (4, 1)), "pcol", 0, 0, tiled=True, axis_index_groups=groups
    )


def from_root(pieces, axis):
    keep = (lambda xi, zi: xi == 0 and zi == 0) if axis == "x" else (lambda xi, zi: zi == 0)
    return [pieces[0]] + [send_from(pieces[n], keep, **{axis: n}) for n in range(1, 4)]


def on_device(matrix, pivots, lower_inverse, upper_inverse):
    prow = lax.axis_index("prow")
    core, x, z = prow % 2, prow // 2 % XS, prow // (2 * XS)
    place = jnp.stack([prow, x, z, core, lax.axis_index("pcol")]).astype(jnp.int32)
    operands = (place, matrix, pivots, lower_inverse, upper_inverse)
    result, most = exchange(*operands)
    return lax.while_loop(
        lambda state: state[0],
        lambda state: (False, exchange_all(*operands)),
        (most >= 2 * HALF, result),
    )[1]


def chip_places(pivots):
    number = lax.broadcasted_iota(jnp.int32, (2 * NB,), 0)
    chip = pivots.reshape(2 * NB) // (2 * ROWS_DEV)
    before = number[None, :] < number[:, None]
    return chip, jnp.sum(jnp.where(before & (chip[None, :] == chip[:, None]), 1, 0), axis=1)


def chosen_places(chip, rank, core):
    where = (chip % XS * ZS + chip // XS) * HALF + rank % HALF
    where = jnp.where(rank // HALF == core, where, -1).reshape(2, 1, NB)
    index = lax.broadcasted_iota(jnp.int32, (XS * ZS * HALF, NB), 0)
    steps = [jnp.where(core == 0, where[k], where[1 - k]) for k in range(2)]
    return [(index == step).astype(jnp.bfloat16) for step in steps]


def exchange(place, matrix, pivots, lower_inverse, upper_inverse):
    prow, core = place[0], place[3]

    number = lax.broadcasted_iota(jnp.int32, (2 * NB,), 0)
    entries, count = owned_rows(pivots, prow, number)
    mine, theirs, panel, top = pick(place, entries, count, matrix)
    parts = panel_parts(panel)
    theirs, pivots = sync(theirs, pivots)
    chip, rank = chip_places(pivots)
    summed = add([mine, send(theirs, core=1)], XS)
    received = [send(summed[j], x=j) for j in range(1, XS)]

    other = send_from(top, lambda xi, zi: xi == 0 and zi == 0, core=1)
    picks = chosen_places(chip, rank, core)
    quarters = spread(place, top, other, picks, summed[:1])
    total = add([summed[0]] + received, ZS)
    *total, parts = sync(*total, parts)

    received = [send(total[k], z=k) for k in range(1, ZS)]
    near_rows = along_y(parts)
    across = lax.ppermute(parts, "pcol", [(n, (n + 4) % 8) for n in range(8)])
    total, across, *quarters = sync(add([total[0]] + received, 1)[0], across, *quarters)

    blocks = gather_z(total)
    near_rows, columns = sync(near_rows, total[:, :NB])
    from_0, from_1 = to_columns(columns)
    crossed = jnp.where(core == 0, from_1, from_0)
    subs = choose(place, 1, from_root(quarters, "x"), ZS, [])
    values = sync(*blocks, crossed, across, *subs)
    blocks, crossed, across, subs = values[:ZS], values[ZS], values[ZS + 1], values[ZS + 2:]
    far_rows = along_y(across)

    (displaced,) = choose(place, 2, from_root(subs, "z"), 1, [])
    total, displaced = sync(pack([blocks, gather_z(crossed)]), displaced)

    total = gather_x(total)
    near_rows, far_rows, columns = sync(near_rows, far_rows, displaced[:, :NB])
    displaced = pack([[displaced]] + [[part] for part in to_columns(columns)])
    displaced = [displaced, send(displaced, core=1)]
    entries, _ = owned_rows(pivots, prow, rank)
    result = update(
        True, place, entries, count, matrix, near_rows, far_rows, lower_inverse, upper_inverse,
        total, displaced,
    )
    return result, jnp.max(rank)


def exchange_all(place, matrix, pivots, lower_inverse, upper_inverse):
    prow, x, z, core, pcol = [place[i] for i in range(5)]
    number = lax.broadcasted_iota(jnp.int32, (2 * NB,), 0)
    entries, count = owned_rows(pivots, prow, number)
    mine, theirs, panel, top = pick(place, entries, count, matrix)
    parts = panel_parts(panel)
    panels = lax.all_to_all(jnp.tile(parts, (8, 1)), "pcol", 0, 0, tiled=True)
    panels = panels.reshape(2, 4 * PART, 2 * NB)
    near = pcol < 4
    near_rows = jnp.where(near, panels[0], panels[1])
    far_rows = jnp.where(near, panels[1], panels[0])

    total = add([mine, send(theirs, core=1)], XS)
    total = add([total[0]] + [send(total[j], x=j) for j in range(1, XS)], ZS)
    (total,) = add([total[0]] + [send(total[k], z=k) for k in range(1, ZS)], 1)
    displaced = choose(place, 1, from_root(add([top], XS), "x"), ZS, [])
    (displaced,) = choose(place, 2, from_root(displaced, "z"), 1, [])

    columns = jnp.concatenate([total[:, :NB], displaced[:, :NB]], axis=0)
    from_0, from_1 = to_columns(columns)
    crossed = jnp.where(core == 0, from_1[:SUB], from_0[:SUB])
    held = pack([[total], [crossed], [displaced], [from_0[SUB:]], [from_1[SUB:]]])
    held = pack([gather_z(held)])
    held = pack([[held] + [send(held, x=j) for j in range(1, XS)]])
    both = [held, send(held, core=1)]
    pieces = [h[j * QUARTER:(j + 1) * QUARTER] for h in both for j in range(XS)]
    wide = COLS_DEV + NB
    return update(
        False, place, entries, count, matrix, near_rows, far_rows, lower_inverse, upper_inverse,
        [piece[:, :wide] for piece in pieces], [piece[:, wide:] for piece in pieces],
    )


def solution(mesh):
    in_specs = (P("prow", "pcol"), P(), P(), P())
    out_specs = P("prow", "pcol")
    return jax.shard_map(
        on_device, mesh=mesh, in_specs=in_specs, out_specs=out_specs, check_vma=False
    )
```

profile of v0, /device:TPU:1, one launch (start us, length us, event | category | flops | bytes accessed | tf_op | source)
XLA Modules:
  0.0 163.3 jit_solution(18081572769930730755)
XLA Ops:
  1.8 4.2 %pick_rows.3 = (f32[256,1024]{1,0:T(8,128)S(1)}, f32[256,1024]{1,0:T(8,128)S(1)}, f32[1280,256]{1,0:T(8,128)}, f32[256,1024]{1,0:T(8,128)S(1)}) custom-call(s32[5]{0:T(128)S(1)} %stack.23.place, s32[512]{0:T(512)S(1)} %select_reduce_fusion.6.entries, s32[1]{0:T(128)} %bitcast.12.count, f32[1280,1024]{1,0:T(8,128)} %a_ref.3), custom_call_target="tpu_custom_call" | custom-call | tf_op jit(solution)/shard_map/pick_rows/pallas_call | solution.py:101
  6.1 6.4 %all-to-all-start.3 = ((f32[8,160,256]{2,1,0:T(8,128)}), f32[8,160,256]{2,1,0:T(8,128)}, u32[]{:S(2)}, u32[]{:S(2)}) async-start(f32[8,160,256]{2,1,0:T(8,128)} %bitcast.13), calls=%async_computation.3 | async-start | bytes 2621440 | tf_op jit(solution)/shard_map/all_to_all | solution.py:422
  18.4 2.5 %collective-permute-start.22 = (f32[64,1024]{1,0:T(8,128)S(1)}, f32[64,1024]{1,0:T(8,128)S(1)}, u32[]{:S(2)}, u32[]{:S(2)}) collective-permute-start(f32[64,1024]{1,0:T(8,128)S(1)} %get-tuple-element.131), channel_id=1, source_target_pairs={{0,32},{8,40},{16,48},{24,56},{32,0},{40,8},{48,16},{56,24},{64,96... | collective-permute-start | bytes 786440 | tf_op jit(solution)/shard_map/ppermute | solution.py:33
  22.3 3.9 %collective-permute-done.21.refs_1_ = f32[64,1024]{1,0:T(8,128)S(1)} collective-permute-done((f32[64,1024]{1,0:T(8,128)S(1)}, f32[64,1024]{1,0:T(8,128)S(1)}, u32[]{:S(2)}, u32[]{:S(2)}) %collective-permute-start.21) | collective-permute-done | bytes 262176 | tf_op jit(solution)/shard_map/ppermute | solution.py:33
  26.2 6.3 %collective-permute-done.22.refs_2_ = f32[64,1024]{1,0:T(8,128)S(1)} collective-permute-done((f32[64,1024]{1,0:T(8,128)S(1)}, f32[64,1024]{1,0:T(8,128)S(1)}, u32[]{:S(2)}, u32[]{:S(2)}) %collective-permute-start.22) | collective-permute-done | bytes 262176 | tf_op jit(solution)/shard_map/ppermute | solution.py:33
  35.5 4.5 %all-to-all-start.4 = ((f32[4,160,512]{2,1,0:T(8,128)}), f32[4,160,512]{2,1,0:T(8,128)S(1)}, u32[]{:S(2)}, u32[]{:S(2)}) async-start(f32[4,160,512]{2,1,0:T(8,128)} %tile.12), calls=%async_computation.4 | async-start | bytes 2621440 | tf_op jit(solution)/shard_map/all_to_all | solution.py:428
  42.0 3.3 %collective-permute-start.24 = (f32[16,1024]{1,0:T(8,128)}, f32[16,1024]{1,0:T(8,128)S(1)}, u32[]{:S(2)}, u32[]{:S(2)}) collective-permute-start(f32[16,1024]{1,0:T(8,128)} %get-tuple-element.140), channel_id=1, source_target_pairs={{0,64},{8,72},{16,80},{24,88},{32,96},{40,104},{48,112},{56,120},{... | collective-permute-start | bytes 196616 | tf_op jit(solution)/shard_map/ppermute | solution.py:33
  45.2 4.1 %collective-permute-start.25 = (f32[16,1024]{1,0:T(8,128)}, f32[16,1024]{1,0:T(8,128)S(1)}, u32[]{:S(2)}, u32[]{:S(2)}) collective-permute-start(f32[16,1024]{1,0:T(8,128)} %get-tuple-element.141), channel_id=1, source_target_pairs={{0,128},{8,136},{16,144},{24,152},{32,160},{40,168},{48,176},{56,1... | collective-permute-start | bytes 196616 | tf_op jit(solution)/shard_map/ppermute | solution.py:33
  49.3 2.3 %collective-permute-start.26 = (f32[16,1024]{1,0:T(8,128)}, f32[16,1024]{1,0:T(8,128)S(1)}, u32[]{:S(2)}, u32[]{:S(2)}) collective-permute-start(f32[16,1024]{1,0:T(8,128)} %get-tuple-element.142), channel_id=1, source_target_pairs={{0,192},{8,200},{16,208},{24,216},{32,224},{40,232},{48,240},{56,2... | collective-permute-start | bytes 196616 | tf_op jit(solution)/shard_map/ppermute | solution.py:33
  52.7 4.3 %spread_rows.1 = (f32[128,1024]{1,0:T(8,128)S(1)}, f32[128,1024]{1,0:T(8,128)}, f32[128,1024]{1,0:T(8,128)}, f32[128,1024]{1,0:T(8,128)}) custom-call(s32[5]{0:T(128)S(1)} %stack.23.place, f32[256,1024]{1,0:T(8,128)S(1)} %get-tuple-element.143.own_ref, f32[256,1024]{1,0:T(8,128)} %collective-permute-done.28.other_ref, bf16[512,256]{1,0:T(8,128)(2,1)S(1)} %fusion.4.pick_own, ...), custom_call_target="tpu_custom_call" | custom-call | tf_op jit(solution)/shard_map/spread_rows/pallas_call | solution.py:156
  58.4 2.9 %collective-permute-start.32 = (f32[128,1024]{1,0:T(8,128)}, f32[128,1024]{1,0:T(8,128)S(1)}, u32[]{:S(2)}, u32[]{:S(2)}) collective-permute-start(f32[128,1024]{1,0:T(8,128)} %get-tuple-element.153), channel_id=1, source_target_pairs={{0,16},{8,24},{1,17},{9,25},{2,18},{10,26},{3,19},{11,27},{4,20},{... | collective-permute-start | bytes 1572872 | tf_op jit(solution)/shard_map/ppermute | solution.py:38
  61.3 2.2 %collective-permute-start.33 = (f32[128,1024]{1,0:T(8,128)}, f32[128,1024]{1,0:T(8,128)}, u32[]{:S(2)}, u32[]{:S(2)}) collective-permute-start(f32[128,1024]{1,0:T(8,128)} %get-tuple-element.154), channel_id=1, source_target_pairs={{0,32},{8,40},{1,33},{9,41},{2,34},{10,42},{3,35},{11,43},{4,36},{... | collective-permute-start | bytes 1572872 | tf_op jit(solution)/shard_map/ppermute | solution.py:38
  63.5 3.2 %collective-permute-start.34 = (f32[128,1024]{1,0:T(8,128)}, f32[128,1024]{1,0:T(8,128)}, u32[]{:S(2)}, u32[]{:S(2)}) collective-permute-start(f32[128,1024]{1,0:T(8,128)} %get-tuple-element.155), channel_id=1, source_target_pairs={{0,48},{8,56},{1,49},{9,57},{2,50},{10,58},{3,51},{11,59},{4,52},{... | collective-permute-start | bytes 1572872 | tf_op jit(solution)/shard_map/ppermute | solution.py:38
  67.3 4.1 %all-to-all-start.5 = ((f32[8,16,256]{2,1,0:T(8,128)}), f32[8,16,256]{2,1,0:T(8,128)S(1)}, u32[]{:S(2)}, u32[]{:S(2)}) async-start(f32[8,16,256]{2,1,0:T(8,128)} %tile.13), calls=%async_computation.5 | async-start | bytes 262144 | tf_op jit(solution)/shard_map/all_to_all | solution.py:417
  71.5 3.5 %collective-permute-start.31 = (f32[16,1024]{1,0:T(8,128)S(1)}, f32[16,1024]{1,0:T(8,128)S(1)}, u32[]{:S(2)}, u32[]{:S(2)}) collective-permute-start(f32[16,1024]{1,0:T(8,128)S(1)} %get-tuple-element.148.refs_0_), channel_id=1, source_target_pairs={{0,192},{8,200},{16,208},{24,216},{32,224},{40,232},{48,240},{56,2... | collective-permute-start | bytes 196616 | tf_op jit(solution)/shard_map/ppermute | solution.py:33
  75.0 5.8 %collective-permute-done.33.refs_2_ = f32[128,1024]{1,0:T(8,128)} collective-permute-done((f32[128,1024]{1,0:T(8,128)}, f32[128,1024]{1,0:T(8,128)}, u32[]{:S(2)}, u32[]{:S(2)}) %collective-permute-start.33) | collective-permute-done | bytes 524320 | tf_op jit(solution)/shard_map/ppermute | solution.py:38
  84.1 3.8 %all-to-all-start.6 = ((f32[4,160,512]{2,1,0:T(8,128)}), f32[4,160,512]{2,1,0:T(8,128)S(1)}, u32[]{:S(2)}, u32[]{:S(2)}) async-start(f32[4,160,512]{2,1,0:T(8,128)} %tile.14), calls=%async_computation.6 | async-start | bytes 2621440 | tf_op jit(solution)/shard_map/all_to_all | solution.py:428
  87.9 2.1 %collective-permute-start.38 = (f32[32,1024]{1,0:T(8,128)}, f32[32,1024]{1,0:T(8,128)S(1)}, u32[]{:S(2)}, u32[]{:S(2)}) collective-permute-start(f32[32,1024]{1,0:T(8,128)} %get-tuple-element.167), channel_id=1, source_target_pairs={{0,64},{8,72},{16,80},{24,88},{32,96},{40,104},{48,112},{56,120},{... | collective-permute-start | bytes 393224 | tf_op jit(solution)/shard_map/ppermute | solution.py:38
  93.4 4.0 %collective-permute-done.35.refs_5_ = f32[16,256]{1,0:T(8,128)S(1)} collective-permute-done((f32[16,256]{1,0:T(8,128)S(1)}, f32[16,256]{1,0:T(8,128)S(1)}, u32[]{:S(2)}, u32[]{:S(2)}) %collective-permute-start.35) | collective-permute-done | bytes 16416 | tf_op jit(solution)/shard_map/ppermute | solution.py:33
  106.0 6.3 %all-to-all-start.7 = ((f32[8,32,256]{2,1,0:T(8,128)}), f32[8,32,256]{2,1,0:T(8,128)S(1)}, u32[]{:S(2)}, u32[]{:S(2)}) async-start(f32[8,32,256]{2,1,0:T(8,128)} %tile.15), calls=%async_computation.7 | async-start | bytes 524288 | tf_op jit(solution)/shard_map/all_to_all | solution.py:417
  115.4 8.2 %collective-permute-start.44 = (f32[64,1280]{1,0:T(8,128)S(1)}, f32[64,1280]{1,0:T(8,128)}, u32[]{:S(2)}, u32[]{:S(2)}) collective-permute-start(f32[64,1280]{1,0:T(8,128)S(1)} %get-tuple-element.173.refs_0_), channel_id=1, source_target_pairs={{0,8},{8,0},{16,24},{24,16},{32,40},{40,32},{48,56},{56,48},{64,72... | collective-permute-start | bytes 983048 | tf_op jit(solution)/shard_map/ppermute | solution.py:33
  123.6 8.3 %collective-permute-start.45 = (f32[64,1280]{1,0:T(8,128)}, f32[64,1280]{1,0:T(8,128)}, u32[]{:S(2)}, u32[]{:S(2)}) collective-permute-start(f32[64,1280]{1,0:T(8,128)} %collective-permute-done.41.refs_1_), channel_id=1, source_target_pairs={{0,8},{8,0},{16,24},{24,16},{32,40},{40,32},{48,56},{56,48},{64,72... | collective-permute-start | bytes 983048 | tf_op jit(solution)/shard_map/ppermute | solution.py:33
  132.8 14.3 %collective-permute-start.48 = (f32[32,1536]{1,0:T(8,128)S(1)}, f32[32,1536]{1,0:T(8,128)S(1)}, u32[]{:S(2)}, u32[]{:S(2)}) collective-permute-start(f32[32,1536]{1,0:T(8,128)S(1)} %pack_blocks.9.refs_8_), channel_id=1, source_target_pairs={{0,8},{8,0},{16,24},{24,16},{32,40},{40,32},{48,56},{56,48},{64,72... | collective-permute-start | bytes 589832 | tf_op jit(solution)/shard_map/ppermute | solution.py:33
  148.6 14.5 %panel_update.3 = f32[1280,1024]{1,0:T(8,128)} custom-call(s32[5]{0:T(128)S(1)} %stack.23.place, s32[512]{0:T(512)S(1)} %select_reduce_fusion.3.entries, s32[1]{0:T(128)} %bitcast.12.count, f32[1280,1024]{1,0:T(8,128)} %a_ref.3, f32[640,512]{1,0:T(8,128)S(1)} %get-tuple-element.171.near_ref, f32[640,512]{1,0:T(8,128)S(1)} %get-tuple-element.172.far_ref, ...), custom_call_target="tpu_custom_call" | custom-call | tf_op jit(solution)/shard_map/panel_update/pallas_call | solution.py:322
  (123 shorter events, 37.1 us)
Async XLA Ops:
  6.1 27.1 %all-to-all-start.3 = ((f32[8,160,256]{2,1,0:T(8,128)}), f32[8,160,256]{2,1,0:T(8,128)}, u32[]{:S(2)}, u32[]{:S(2)}) async-start(f32[8,160,256]{2,1,0:T(8,128)} %bitcast.13), calls=%async_computation.3 | async-start | bytes 2621440 | tf_op jit(solution)/shard_map/all_to_all | solution.py:422
  14.7 37.1 %collective-permute-start.28 = (f32[256,1024]{1,0:T(8,128)S(1)}, f32[256,1024]{1,0:T(8,128)}, u32[]{:S(2)}, u32[]{:S(2)}) collective-permute-start(f32[256,1024]{1,0:T(8,128)S(1)} %get-tuple-element.143.own_ref), channel_id=1, source_target_pairs={{0,8},{8,0},{1,9},{9,1},{2,10},{10,2},{3,11},{11,3},{4,12},{12,4},... | collective-permute-start | bytes 3145736 | tf_op jit(solution)/shard_map/ppermute | solution.py:38
  18.4 14.1 %collective-permute-start.22 = (f32[64,1024]{1,0:T(8,128)S(1)}, f32[64,1024]{1,0:T(8,128)S(1)}, u32[]{:S(2)}, u32[]{:S(2)}) collective-permute-start(f32[64,1024]{1,0:T(8,128)S(1)} %get-tuple-element.131), channel_id=1, source_target_pairs={{0,32},{8,40},{16,48},{24,56},{32,0},{40,8},{48,16},{56,24},{64,96... | collective-permute-start | bytes 786440 | tf_op jit(solution)/shard_map/ppermute | solution.py:33
  20.8 11.7 %collective-permute-start.23 = (f32[64,1024]{1,0:T(8,128)S(1)}, f32[64,1024]{1,0:T(8,128)S(1)}, u32[]{:S(2)}, u32[]{:S(2)}) collective-permute-start(f32[64,1024]{1,0:T(8,128)S(1)} %get-tuple-element.132), channel_id=1, source_target_pairs={{0,48},{8,56},{16,0},{24,8},{32,16},{40,24},{48,32},{56,40},{64,11... | collective-permute-start | bytes 786440 | tf_op jit(solution)/shard_map/ppermute | solution.py:33
  35.5 31.1 %all-to-all-start.4 = ((f32[4,160,512]{2,1,0:T(8,128)}), f32[4,160,512]{2,1,0:T(8,128)S(1)}, u32[]{:S(2)}, u32[]{:S(2)}) async-start(f32[4,160,512]{2,1,0:T(8,128)} %tile.12), calls=%async_computation.4 | async-start | bytes 2621440 | tf_op jit(solution)/shard_map/all_to_all | solution.py:428
  40.7 17.7 %collective-permute-start.27 = (f32[160,512]{1,0:T(8,128)S(1)}, f32[160,512]{1,0:T(8,128)S(1)}, u32[]{:S(2)}, u32[]{:S(2)}) collective-permute-start(f32[160,512]{1,0:T(8,128)S(1)} %get-tuple-element.138), channel_id=1, source_target_pairs={{0,4},{1,5},{2,6},{3,7},{4,0},{5,1},{6,2},{7,3},{8,12},{9,13},{10,... | collective-permute-start | bytes 983048 | tf_op jit(solution)/shard_map/ppermute | solution.py:486
  42.0 15.0 %collective-permute-start.24 = (f32[16,1024]{1,0:T(8,128)}, f32[16,1024]{1,0:T(8,128)S(1)}, u32[]{:S(2)}, u32[]{:S(2)}) collective-permute-start(f32[16,1024]{1,0:T(8,128)} %get-tuple-element.140), channel_id=1, source_target_pairs={{0,64},{8,72},{16,80},{24,88},{32,96},{40,104},{48,112},{56,120},{... | collective-permute-start | bytes 196616 | tf_op jit(solution)/shard_map/ppermute | solution.py:33
  45.2 13.1 %collective-permute-start.25 = (f32[16,1024]{1,0:T(8,128)}, f32[16,1024]{1,0:T(8,128)S(1)}, u32[]{:S(2)}, u32[]{:S(2)}) collective-permute-start(f32[16,1024]{1,0:T(8,128)} %get-tuple-element.141), channel_id=1, source_target_pairs={{0,128},{8,136},{16,144},{24,152},{32,160},{40,168},{48,176},{56,1... | collective-permute-start | bytes 196616 | tf_op jit(solution)/shard_map/ppermute | solution.py:33
  58.4 13.1 %collective-permute-start.32 = (f32[128,1024]{1,0:T(8,128)}, f32[128,1024]{1,0:T(8,128)S(1)}, u32[]{:S(2)}, u32[]{:S(2)}) collective-permute-start(f32[128,1024]{1,0:T(8,128)} %get-tuple-element.153), channel_id=1, source_target_pairs={{0,16},{8,24},{1,17},{9,25},{2,18},{10,26},{3,19},{11,27},{4,20},{... | collective-permute-start | bytes 1572872 | tf_op jit(solution)/shard_map/ppermute | solution.py:38
  61.3 19.5 %collective-permute-start.33 = (f32[128,1024]{1,0:T(8,128)}, f32[128,1024]{1,0:T(8,128)}, u32[]{:S(2)}, u32[]{:S(2)}) collective-permute-start(f32[128,1024]{1,0:T(8,128)} %get-tuple-element.154), channel_id=1, source_target_pairs={{0,32},{8,40},{1,33},{9,41},{2,34},{10,42},{3,35},{11,43},{4,36},{... | collective-permute-start | bytes 1572872 | tf_op jit(solution)/shard_map/ppermute | solution.py:38
  63.5 17.3 %collective-permute-start.34 = (f32[128,1024]{1,0:T(8,128)}, f32[128,1024]{1,0:T(8,128)}, u32[]{:S(2)}, u32[]{:S(2)}) collective-permute-start(f32[128,1024]{1,0:T(8,128)} %get-tuple-element.155), channel_id=1, source_target_pairs={{0,48},{8,56},{1,49},{9,57},{2,50},{10,58},{3,51},{11,59},{4,52},{... | collective-permute-start | bytes 1572872 | tf_op jit(solution)/shard_map/ppermute | solution.py:38
  67.3 15.4 %all-to-all-start.5 = ((f32[8,16,256]{2,1,0:T(8,128)}), f32[8,16,256]{2,1,0:T(8,128)S(1)}, u32[]{:S(2)}, u32[]{:S(2)}) async-start(f32[8,16,256]{2,1,0:T(8,128)} %tile.13), calls=%async_computation.5 | async-start | bytes 262144 | tf_op jit(solution)/shard_map/all_to_all | solution.py:417
  84.1 21.1 %all-to-all-start.6 = ((f32[4,160,512]{2,1,0:T(8,128)}), f32[4,160,512]{2,1,0:T(8,128)S(1)}, u32[]{:S(2)}, u32[]{:S(2)}) async-start(f32[4,160,512]{2,1,0:T(8,128)} %tile.14), calls=%async_computation.6 | async-start | bytes 2621440 | tf_op jit(solution)/shard_map/all_to_all | solution.py:428
  87.9 15.8 %collective-permute-start.38 = (f32[32,1024]{1,0:T(8,128)}, f32[32,1024]{1,0:T(8,128)S(1)}, u32[]{:S(2)}, u32[]{:S(2)}) collective-permute-start(f32[32,1024]{1,0:T(8,128)} %get-tuple-element.167), channel_id=1, source_target_pairs={{0,64},{8,72},{16,80},{24,88},{32,96},{40,104},{48,112},{56,120},{... | collective-permute-start | bytes 393224 | tf_op jit(solution)/shard_map/ppermute | solution.py:38
  90.0 13.7 %collective-permute-start.39 = (f32[32,1024]{1,0:T(8,128)}, f32[32,1024]{1,0:T(8,128)S(1)}, u32[]{:S(2)}, u32[]{:S(2)}) collective-permute-start(f32[32,1024]{1,0:T(8,128)} %get-tuple-element.168), channel_id=1, source_target_pairs={{0,128},{8,136},{16,144},{24,152},{32,160},{40,168},{48,176},{56,1... | collective-permute-start | bytes 393224 | tf_op jit(solution)/shard_map/ppermute | solution.py:38
  91.3 12.4 %collective-permute-start.40 = (f32[32,1024]{1,0:T(8,128)}, f32[32,1024]{1,0:T(8,128)S(1)}, u32[]{:S(2)}, u32[]{:S(2)}) collective-permute-start(f32[32,1024]{1,0:T(8,128)} %get-tuple-element.169), channel_id=1, source_target_pairs={{0,192},{8,200},{16,208},{24,216},{32,224},{40,232},{48,240},{56,2... | collective-permute-start | bytes 393224 | tf_op jit(solution)/shard_map/ppermute | solution.py:38
  106.0 26.8 %all-to-all-start.7 = ((f32[8,32,256]{2,1,0:T(8,128)}), f32[8,32,256]{2,1,0:T(8,128)S(1)}, u32[]{:S(2)}, u32[]{:S(2)}) async-start(f32[8,32,256]{2,1,0:T(8,128)} %tile.15), calls=%async_computation.7 | async-start | bytes 524288 | tf_op jit(solution)/shard_map/all_to_all | solution.py:417
  112.3 19.5 %collective-permute-start.42 = (f32[64,1280]{1,0:T(8,128)S(1)}, f32[64,1280]{1,0:T(8,128)}, u32[]{:S(2)}, u32[]{:S(2)}) collective-permute-start(f32[64,1280]{1,0:T(8,128)S(1)} %get-tuple-element.173.refs_0_), channel_id=1, source_target_pairs={{0,32},{8,40},{16,48},{24,56},{32,0},{40,8},{48,16},{56,24},{64,96... | collective-permute-start | bytes 983048 | tf_op jit(solution)/shard_map/ppermute | solution.py:33
  113.3 18.6 %collective-permute-start.43 = (f32[64,1280]{1,0:T(8,128)S(1)}, f32[64,1280]{1,0:T(8,128)}, u32[]{:S(2)}, u32[]{:S(2)}) collective-permute-start(f32[64,1280]{1,0:T(8,128)S(1)} %get-tuple-element.173.refs_0_), channel_id=1, source_target_pairs={{0,48},{8,56},{16,0},{24,8},{32,16},{40,24},{48,32},{56,40},{64,11... | collective-permute-start | bytes 983048 | tf_op jit(solution)/shard_map/ppermute | solution.py:33
  115.4 32.6 %collective-permute-start.44 = (f32[64,1280]{1,0:T(8,128)S(1)}, f32[64,1280]{1,0:T(8,128)}, u32[]{:S(2)}, u32[]{:S(2)}) collective-permute-start(f32[64,1280]{1,0:T(8,128)S(1)} %get-tuple-element.173.refs_0_), channel_id=1, source_target_pairs={{0,8},{8,0},{16,24},{24,16},{32,40},{40,32},{48,56},{56,48},{64,72... | collective-permute-start | bytes 983048 | tf_op jit(solution)/shard_map/ppermute | solution.py:33
  123.6 24.4 %collective-permute-start.45 = (f32[64,1280]{1,0:T(8,128)}, f32[64,1280]{1,0:T(8,128)}, u32[]{:S(2)}, u32[]{:S(2)}) collective-permute-start(f32[64,1280]{1,0:T(8,128)} %collective-permute-done.41.refs_1_), channel_id=1, source_target_pairs={{0,8},{8,0},{16,24},{24,16},{32,40},{40,32},{48,56},{56,48},{64,72... | collective-permute-start | bytes 983048 | tf_op jit(solution)/shard_map/ppermute | solution.py:33
  131.9 16.1 %collective-permute-start.46 = (f32[64,1280]{1,0:T(8,128)}, f32[64,1280]{1,0:T(8,128)}, u32[]{:S(2)}, u32[]{:S(2)}) collective-permute-start(f32[64,1280]{1,0:T(8,128)} %collective-permute-done.42.refs_2_), channel_id=1, source_target_pairs={{0,8},{8,0},{16,24},{24,16},{32,40},{40,32},{48,56},{56,48},{64,72... | collective-permute-start | bytes 983048 | tf_op jit(solution)/shard_map/ppermute | solution.py:33
  131.9 16.1 %collective-permute-start.47 = (f32[64,1280]{1,0:T(8,128)}, f32[64,1280]{1,0:T(8,128)}, u32[]{:S(2)}, u32[]{:S(2)}) collective-permute-start(f32[64,1280]{1,0:T(8,128)} %collective-permute-done.43.refs_3_), channel_id=1, source_target_pairs={{0,8},{8,0},{16,24},{24,16},{32,40},{40,32},{48,56},{56,48},{64,72... | collective-permute-start | bytes 983048 | tf_op jit(solution)/shard_map/ppermute | solution.py:33
  132.8 15.8 %collective-permute-start.48 = (f32[32,1536]{1,0:T(8,128)S(1)}, f32[32,1536]{1,0:T(8,128)S(1)}, u32[]{:S(2)}, u32[]{:S(2)}) collective-permute-start(f32[32,1536]{1,0:T(8,128)S(1)} %pack_blocks.9.refs_8_), channel_id=1, source_target_pairs={{0,8},{8,0},{16,24},{24,16},{32,40},{40,32},{48,56},{56,48},{64,72... | collective-permute-start | bytes 589832 | tf_op jit(solution)/shard_map/ppermute | solution.py:33
  (24 other events, 122.8 us)
where the time goes:
time: 166 us; the launch traced here: 163 us
  starting transfers between devices  95.6 us (58%)
  Pallas kernels  26.5 us (16%)
  waiting for transfers between devices  26.2 us (16%)
  local copies, waits for them, and re-layouts  10.4 us (6%)
  other arithmetic  3.21 us (2%)
    ppermute x21, starting transfers between devices, send(): return lax.ppermute(value, 'prow', shift(core, x, z))  54.5 us
    ppermute x21, waiting for transfers between devices, send(): return lax.ppermute(value, 'prow', shift(core, x, z))  20.4 us
    ppermute x7, starting transfers between devices, send_from(): return lax.ppermute(value, 'prow', pairs)  14.8 us
    pallas_call x1, Pallas kernels, update(): pl.pallas_call(functools.partial(update_kernel, packed), grid=(ROWS_DEV /...  14.5 us
    all_to_all x2, starting transfers between devices, to_columns(): value = lax.all_to_all(jnp.tile(value, (8, 1)), 'pcol', 0, 0, tiled=True)  10.4 us
    all_to_all x2, starting transfers between devices, along_y(): lax.all_to_all(jnp.tile(parts, (4, 1)), 'pcol', 0, 0, tiled=True, axis_in...  8.31 us
    all_to_all x1, starting transfers between devices, panel_parts(): parts = lax.all_to_all(panel, 'pcol', 0, 0, tiled=True)  6.39 us
    ppermute x7, waiting for transfers between devices, send_from(): return lax.ppermute(value, 'prow', pairs)  5.78 us
  transfers between devices with their start and end apart: 34, of which 9 were waited for; matrix products, arithmetic and copies ran while one was open for 3% of the time, Pallas kernels for 5%

commit v1 on v0

--- a/solution.py
+++ b/solution.py
@@ -482,17 +482,16 @@
     *total, parts = sync(*total, parts)
 
     received = [send(total[k], z=k) for k in range(1, ZS)]
-    near_rows = along_y(parts)
     across = lax.ppermute(parts, "pcol", [(n, (n + 4) % 8) for n in range(8)])
     total, across, *quarters = sync(add([total[0]] + received, 1)[0], across, *quarters)
 
     blocks = gather_z(total)
-    near_rows, columns = sync(near_rows, total[:, :NB])
-    from_0, from_1 = to_columns(columns)
+    from_0, from_1 = to_columns(total[:, :NB])
     crossed = jnp.where(core == 0, from_1, from_0)
     subs = choose(place, 1, from_root(quarters, "x"), ZS, [])
-    values = sync(*blocks, crossed, across, *subs)
-    blocks, crossed, across, subs = values[:ZS], values[ZS], values[ZS + 1], values[ZS + 2:]
+    values = sync(*blocks, crossed, parts, *subs)
+    blocks, crossed, parts, subs = values[:ZS], values[ZS], values[ZS + 1], values[ZS + 2:]
+    near_rows = along_y(parts)
     far_rows = along_y(across)
 
     (displaced,) = choose(place, 2, from_root(subs, "z"), 1, [])

time: 166 us -> 174 us (1.048)
  the two profiles are of different devices: /device:TPU:1 before, /device:TPU:4 now
where the time goes in v1:
time: 174 us; the launch traced here: 171 us
  starting transfers between devices  65.4 us (38%)
  waiting for transfers between devices  54.9 us (32%)
  Pallas kernels  26.2 us (15%)
  blocking collectives  10.7 us (6%)
  local copies, waits for them, and re-layouts  6.87 us (4%)
  other arithmetic  5.07 us (3%)
    ppermute x21, waiting for transfers between devices, send(): return lax.ppermute(value, 'prow', shift(core, x, z))  39.5 us
    ppermute x21, starting transfers between devices, send(): return lax.ppermute(value, 'prow', shift(core, x, z))  37.1 us
    pallas_call x1, Pallas kernels, update(): pl.pallas_call(functools.partial(update_kernel, packed), grid=(ROWS_DEV /...  15.8 us
    ppermute x7, waiting for transfers between devices, send_from(): return lax.ppermute(value, 'prow', pairs)  15.4 us
    all_to_all x1, blocking collectives, to_columns(): value = lax.all_to_all(jnp.tile(value, (8, 1)), 'pcol', 0, 0, tiled=True)  10.7 us
    all_to_all x2, starting transfers between devices, along_y(): lax.all_to_all(jnp.tile(parts, (4, 1)), 'pcol', 0, 0, tiled=True, axis_in...  8.13 us
    ppermute x7, starting transfers between devices, send_from(): return lax.ppermute(value, 'prow', pairs)  7.29 us
    all_to_all x1, starting transfers between devices, panel_parts(): parts = lax.all_to_all(panel, 'pcol', 0, 0, tiled=True)  5.84 us
  transfers between devices with their start and end apart: 33, of which 12 were waited for; matrix products, arithmetic and copies ran while one was open for 3% of the time, Pallas kernels for 3%

profile of v1, /device:TPU:4, one launch (start us, length us, event | category | flops | bytes accessed | tf_op | source)
XLA Modules:
  0.0 170.6 jit_solution(7245435140725066816)
XLA Ops:
  1.8 4.7 %pick_rows.3 = (f32[256,1024]{1,0:T(8,128)S(1)}, f32[256,1024]{1,0:T(8,128)}, f32[1280,256]{1,0:T(8,128)}, f32[256,1024]{1,0:T(8,128)S(1)}) custom-call(s32[5]{0:T(128)S(1)} %stack.23.place, s32[512]{0:T(512)S(1)} %select_reduce_fusion.6.entries, s32[1]{0:T(128)} %bitcast.12.count, f32[1280,1024]{1,0:T(8,128)} %a_ref.3), custom_call_target="tpu_custom_call" | custom-call | tf_op jit(solution)/shard_map/pick_rows/pallas_call | solution.py:101
  6.6 5.8 %all-to-all-start.3 = ((f32[8,160,256]{2,1,0:T(8,128)}), f32[8,160,256]{2,1,0:T(8,128)}, u32[]{:S(2)}, u32[]{:S(2)}) async-start(f32[8,160,256]{2,1,0:T(8,128)} %bitcast.13), calls=%async_computation.3 | async-start | bytes 2621440 | tf_op jit(solution)/shard_map/all_to_all | solution.py:422
  15.5 2.2 %add_parts.11 = (f32[64,1024]{1,0:T(8,128)S(1)}, f32[64,1024]{1,0:T(8,128)}, f32[64,1024]{1,0:T(8,128)}, f32[64,1024]{1,0:T(8,128)}) custom-call(f32[256,1024]{1,0:T(8,128)S(1)} %get-tuple-element.125.refs_0_, f32[256,1024]{1,0:T(8,128)} %collective-permute-done.20.refs_1_), custom_call_target="tpu_custom_call" | custom-call | tf_op jit(solution)/shard_map/add_parts/pallas_call | solution.py:359
  19.5 1.7 collective-permute-start.23
  22.4 9.4 %collective-permute-done.21.refs_1_ = f32[64,1024]{1,0:T(8,128)S(1)} collective-permute-done((f32[64,1024]{1,0:T(8,128)}, f32[64,1024]{1,0:T(8,128)S(1)}, u32[]{:S(2)}, u32[]{:S(2)}) %collective-permute-start.21) | collective-permute-done | bytes 262176 | tf_op jit(solution)/shard_map/ppermute | solution.py:33
  31.8 1.8 %collective-permute-done.23.refs_3_ = f32[64,1024]{1,0:T(8,128)S(1)} collective-permute-done((f32[64,1024]{1,0:T(8,128)}, f32[64,1024]{1,0:T(8,128)S(1)}, u32[]{:S(2)}, u32[]{:S(2)}) %collective-permute-start.23) | collective-permute-done | bytes 262176 | tf_op jit(solution)/shard_map/ppermute | solution.py:33
  35.5 2.1 %collective-permute-start.27 = (f32[160,512]{1,0:T(8,128)S(1)}, f32[160,512]{1,0:T(8,128)S(1)}, u32[]{:S(2)}, u32[]{:S(2)}) collective-permute-start(f32[160,512]{1,0:T(8,128)S(1)} %get-tuple-element.140.refs_5_), channel_id=1, source_target_pairs={{0,4},{1,5},{2,6},{3,7},{4,0},{5,1},{6,2},{7,3},{8,12},{9,13},{10,... | collective-permute-start | bytes 983048 | tf_op jit(solution)/shard_map/ppermute | solution.py:485
  37.6 3.5 %collective-permute-start.24 = (f32[16,1024]{1,0:T(8,128)}, f32[16,1024]{1,0:T(8,128)S(1)}, u32[]{:S(2)}, u32[]{:S(2)}) collective-permute-start(f32[16,1024]{1,0:T(8,128)} %get-tuple-element.137), channel_id=1, source_target_pairs={{0,64},{8,72},{16,80},{24,88},{32,96},{40,104},{48,112},{56,120},{... | collective-permute-start | bytes 196616 | tf_op jit(solution)/shard_map/ppermute | solution.py:33
  41.2 4.2 %collective-permute-start.25 = (f32[16,1024]{1,0:T(8,128)}, f32[16,1024]{1,0:T(8,128)S(1)}, u32[]{:S(2)}, u32[]{:S(2)}) collective-permute-start(f32[16,1024]{1,0:T(8,128)} %get-tuple-element.138), channel_id=1, source_target_pairs={{0,128},{8,136},{16,144},{24,152},{32,160},{40,168},{48,176},{56,1... | collective-permute-start | bytes 196616 | tf_op jit(solution)/shard_map/ppermute | solution.py:33
  45.4 2.6 %collective-permute-start.26 = (f32[16,1024]{1,0:T(8,128)}, f32[16,1024]{1,0:T(8,128)S(1)}, u32[]{:S(2)}, u32[]{:S(2)}) collective-permute-start(f32[16,1024]{1,0:T(8,128)} %get-tuple-element.139), channel_id=1, source_target_pairs={{0,192},{8,200},{16,208},{24,216},{32,224},{40,232},{48,240},{56,2... | collective-permute-start | bytes 196616 | tf_op jit(solution)/shard_map/ppermute | solution.py:33
  48.6 5.1 %collective-permute-done.24.refs_1_ = f32[16,1024]{1,0:T(8,128)S(1)} collective-permute-done((f32[16,1024]{1,0:T(8,128)}, f32[16,1024]{1,0:T(8,128)S(1)}, u32[]{:S(2)}, u32[]{:S(2)}) %collective-permute-start.24) | collective-permute-done | bytes 65568 | tf_op jit(solution)/shard_map/ppermute | solution.py:33
  56.1 10.7 %all_to_all.57 = f32[8,16,256]{2,1,0:T(8,128)} all-to-all(f32[8,16,256]{2,1,0:T(8,128)S(1)} %tile.12), channel_id=1, replica_groups=mesh['prow'=32,'pcol'=8] {'pcol'}, dimensions={0} | all-to-all | bytes 262144 | tf_op jit(solution)/shard_map/all_to_all | solution.py:417
  68.1 3.7 %all-to-all-start.6 = ((f32[4,160,512]{2,1,0:T(8,128)}), f32[4,160,512]{2,1,0:T(8,128)S(1)}, u32[]{:S(2)}, u32[]{:S(2)}) async-start(f32[4,160,512]{2,1,0:T(8,128)} %tile.14), calls=%async_computation.6 | async-start | bytes 2621440 | tf_op jit(solution)/shard_map/all_to_all | solution.py:428
  75.4 2.4 %collective-permute-start.30 = (f32[16,1024]{1,0:T(8,128)S(1)}, f32[16,1024]{1,0:T(8,128)S(1)}, u32[]{:S(2)}, u32[]{:S(2)}) collective-permute-start(f32[16,1024]{1,0:T(8,128)S(1)} %get-tuple-element.146.refs_0_), channel_id=1, source_target_pairs={{0,128},{8,136},{16,144},{24,152},{32,160},{40,168},{48,176},{56,1... | collective-permute-start | bytes 196616 | tf_op jit(solution)/shard_map/ppermute | solution.py:33
  77.9 1.8 %collective-permute-start.31 = (f32[16,1024]{1,0:T(8,128)S(1)}, f32[16,1024]{1,0:T(8,128)S(1)}, u32[]{:S(2)}, u32[]{:S(2)}) collective-permute-start(f32[16,1024]{1,0:T(8,128)S(1)} %get-tuple-element.146.refs_0_), channel_id=1, source_target_pairs={{0,192},{8,200},{16,208},{24,216},{32,224},{40,232},{48,240},{56,2... | collective-permute-start | bytes 196616 | tf_op jit(solution)/shard_map/ppermute | solution.py:33
  80.4 15.3 %collective-permute-done.33.refs_2_ = f32[128,1024]{1,0:T(8,128)S(1)} collective-permute-done((f32[128,1024]{1,0:T(8,128)}, f32[128,1024]{1,0:T(8,128)S(1)}, u32[]{:S(2)}, u32[]{:S(2)}) %collective-permute-start.33) | collective-permute-done | bytes 524320 | tf_op jit(solution)/shard_map/ppermute | solution.py:38
  98.6 4.5 %all-to-all-start.5 = ((f32[4,160,512]{2,1,0:T(8,128)}), f32[4,160,512]{2,1,0:T(8,128)S(1)}, u32[]{:S(2)}, u32[]{:S(2)}) async-start(f32[4,160,512]{2,1,0:T(8,128)} %tile.13), calls=%async_computation.5 | async-start | bytes 2621440 | tf_op jit(solution)/shard_map/all_to_all | solution.py:428
  107.1 5.7 %collective-permute-done.35.refs_5_ = f32[16,256]{1,0:T(8,128)S(1)} collective-permute-done((f32[16,256]{1,0:T(8,128)S(1)}, f32[16,256]{1,0:T(8,128)S(1)}, u32[]{:S(2)}, u32[]{:S(2)}) %collective-permute-start.35) | collective-permute-done | bytes 16416 | tf_op jit(solution)/shard_map/ppermute | solution.py:33
  112.9 1.9 %collective-permute-done.36.refs_6_ = f32[16,256]{1,0:T(8,128)S(1)} collective-permute-done((f32[16,256]{1,0:T(8,128)S(1)}, f32[16,256]{1,0:T(8,128)S(1)}, u32[]{:S(2)}, u32[]{:S(2)}) %collective-permute-start.36) | collective-permute-done | bytes 16416 | tf_op jit(solution)/shard_map/ppermute | solution.py:33
  114.8 2.8 %collective-permute-done.37.refs_7_ = f32[16,256]{1,0:T(8,128)S(1)} collective-permute-done((f32[16,256]{1,0:T(8,128)S(1)}, f32[16,256]{1,0:T(8,128)S(1)}, u32[]{:S(2)}, u32[]{:S(2)}) %collective-permute-start.37) | collective-permute-done | bytes 16416 | tf_op jit(solution)/shard_map/ppermute | solution.py:33
  120.8 5.0 %all-to-all-start.7 = ((f32[8,32,256]{2,1,0:T(8,128)}), f32[8,32,256]{2,1,0:T(8,128)S(1)}, u32[]{:S(2)}, u32[]{:S(2)}) async-start(f32[8,32,256]{2,1,0:T(8,128)} %tile.15), calls=%async_computation.7 | async-start | bytes 524288 | tf_op jit(solution)/shard_map/all_to_all | solution.py:417
  128.3 8.1 %collective-permute-done.41.refs_1_ = f32[64,1280]{1,0:T(8,128)} collective-permute-done((f32[64,1280]{1,0:T(8,128)S(1)}, f32[64,1280]{1,0:T(8,128)}, u32[]{:S(2)}, u32[]{:S(2)}) %collective-permute-start.41) | collective-permute-done | bytes 327712 | tf_op jit(solution)/shard_map/ppermute | solution.py:33
  138.6 14.9 %collective-permute-start.48 = (f32[32,1536]{1,0:T(8,128)S(1)}, f32[32,1536]{1,0:T(8,128)S(1)}, u32[]{:S(2)}, u32[]{:S(2)}) collective-permute-start(f32[32,1536]{1,0:T(8,128)S(1)} %pack_blocks.9.refs_8_), channel_id=1, source_target_pairs={{0,8},{8,0},{16,24},{24,16},{32,40},{40,32},{48,56},{56,48},{64,72... | collective-permute-start | bytes 589832 | tf_op jit(solution)/shard_map/ppermute | solution.py:33
  154.5 15.8 %panel_update.3 = f32[1280,1024]{1,0:T(8,128)} custom-call(s32[5]{0:T(128)S(1)} %copy-done.31, s32[512]{0:T(512)S(1)} %select_reduce_fusion.3.entries, s32[1]{0:T(128)} %bitcast.12.count, f32[1280,1024]{1,0:T(8,128)} %a_ref.3, f32[640,512]{1,0:T(8,128)S(1)} %get-tuple-element.167.near_ref, f32[640,512]{1,0:T(8,128)S(1)} %get-tuple-element.168.far_ref, ...), custom_call_target="tpu_custom_call" | custom-call | tf_op jit(solution)/shard_map/panel_update/pallas_call | solution.py:322
  (123 shorter events, 33.5 us)
Async XLA Ops:
  6.6 27.8 %all-to-all-start.3 = ((f32[8,160,256]{2,1,0:T(8,128)}), f32[8,160,256]{2,1,0:T(8,128)}, u32[]{:S(2)}, u32[]{:S(2)}) async-start(f32[8,160,256]{2,1,0:T(8,128)} %bitcast.13), calls=%async_computation.3 | async-start | bytes 2621440 | tf_op jit(solution)/shard_map/all_to_all | solution.py:422
  12.5 35.5 %collective-permute-start.28 = (f32[256,1024]{1,0:T(8,128)S(1)}, f32[256,1024]{1,0:T(8,128)S(1)}, u32[]{:S(2)}, u32[]{:S(2)}) collective-permute-start(f32[256,1024]{1,0:T(8,128)S(1)} %get-tuple-element.141.own_ref), channel_id=1, source_target_pairs={{0,8},{8,0},{1,9},{9,1},{2,10},{10,2},{3,11},{11,3},{4,12},{12,4},... | collective-permute-start | bytes 3145736 | tf_op jit(solution)/shard_map/ppermute | solution.py:38
  17.7 14.2 %collective-permute-start.21 = (f32[64,1024]{1,0:T(8,128)}, f32[64,1024]{1,0:T(8,128)S(1)}, u32[]{:S(2)}, u32[]{:S(2)}) collective-permute-start(f32[64,1024]{1,0:T(8,128)} %get-tuple-element.128), channel_id=1, source_target_pairs={{0,16},{8,24},{16,32},{24,40},{32,48},{40,56},{48,0},{56,8},{64,80... | collective-permute-start | bytes 786440 | tf_op jit(solution)/shard_map/ppermute | solution.py:33
  18.7 13.2 %collective-permute-start.22 = (f32[64,1024]{1,0:T(8,128)}, f32[64,1024]{1,0:T(8,128)S(1)}, u32[]{:S(2)}, u32[]{:S(2)}) collective-permute-start(f32[64,1024]{1,0:T(8,128)} %get-tuple-element.129), channel_id=1, source_target_pairs={{0,32},{8,40},{16,48},{24,56},{32,0},{40,8},{48,16},{56,24},{64,96... | collective-permute-start | bytes 786440 | tf_op jit(solution)/shard_map/ppermute | solution.py:33
  19.5 14.2 %collective-permute-start.23 = (f32[64,1024]{1,0:T(8,128)}, f32[64,1024]{1,0:T(8,128)S(1)}, u32[]{:S(2)}, u32[]{:S(2)}) collective-permute-start(f32[64,1024]{1,0:T(8,128)} %get-tuple-element.130), channel_id=1, source_target_pairs={{0,48},{8,56},{16,0},{24,8},{32,16},{40,24},{48,32},{56,40},{64,11... | collective-permute-start | bytes 786440 | tf_op jit(solution)/shard_map/ppermute | solution.py:33
  35.5 19.8 %collective-permute-start.27 = (f32[160,512]{1,0:T(8,128)S(1)}, f32[160,512]{1,0:T(8,128)S(1)}, u32[]{:S(2)}, u32[]{:S(2)}) collective-permute-start(f32[160,512]{1,0:T(8,128)S(1)} %get-tuple-element.140.refs_5_), channel_id=1, source_target_pairs={{0,4},{1,5},{2,6},{3,7},{4,0},{5,1},{6,2},{7,3},{8,12},{9,13},{10,... | collective-permute-start | bytes 983048 | tf_op jit(solution)/shard_map/ppermute | solution.py:485
  37.6 16.0 %collective-permute-start.24 = (f32[16,1024]{1,0:T(8,128)}, f32[16,1024]{1,0:T(8,128)S(1)}, u32[]{:S(2)}, u32[]{:S(2)}) collective-permute-start(f32[16,1024]{1,0:T(8,128)} %get-tuple-element.137), channel_id=1, source_target_pairs={{0,64},{8,72},{16,80},{24,88},{32,96},{40,104},{48,112},{56,120},{... | collective-permute-start | bytes 196616 | tf_op jit(solution)/shard_map/ppermute | solution.py:33
  41.2 14.1 %collective-permute-start.25 = (f32[16,1024]{1,0:T(8,128)}, f32[16,1024]{1,0:T(8,128)S(1)}, u32[]{:S(2)}, u32[]{:S(2)}) collective-permute-start(f32[16,1024]{1,0:T(8,128)} %get-tuple-element.138), channel_id=1, source_target_pairs={{0,128},{8,136},{16,144},{24,152},{32,160},{40,168},{48,176},{56,1... | collective-permute-start | bytes 196616 | tf_op jit(solution)/shard_map/ppermute | solution.py:33
  68.1 29.3 %all-to-all-start.6 = ((f32[4,160,512]{2,1,0:T(8,128)}), f32[4,160,512]{2,1,0:T(8,128)S(1)}, u32[]{:S(2)}, u32[]{:S(2)}) async-start(f32[4,160,512]{2,1,0:T(8,128)} %tile.14), calls=%async_computation.6 | async-start | bytes 2621440 | tf_op jit(solution)/shard_map/all_to_all | solution.py:428
  72.4 23.3 %collective-permute-start.33 = (f32[128,1024]{1,0:T(8,128)}, f32[128,1024]{1,0:T(8,128)S(1)}, u32[]{:S(2)}, u32[]{:S(2)}) collective-permute-start(f32[128,1024]{1,0:T(8,128)} %copy-done.21), channel_id=1, source_target_pairs={{0,32},{8,40},{1,33},{9,41},{2,34},{10,42},{3,35},{11,43},{4,36},{... | collective-permute-start | bytes 1572872 | tf_op jit(solution)/shard_map/ppermute | solution.py:38
  73.7 22.0 %collective-permute-start.34 = (f32[128,1024]{1,0:T(8,128)}, f32[128,1024]{1,0:T(8,128)S(1)}, u32[]{:S(2)}, u32[]{:S(2)}) collective-permute-start(f32[128,1024]{1,0:T(8,128)} %copy-done.22), channel_id=1, source_target_pairs={{0,48},{8,56},{1,49},{9,57},{2,50},{10,58},{3,51},{11,59},{4,52},{... | collective-permute-start | bytes 1572872 | tf_op jit(solution)/shard_map/ppermute | solution.py:38
  74.4 22.9 %collective-permute-start.29 = (f32[16,1024]{1,0:T(8,128)S(1)}, f32[16,1024]{1,0:T(8,128)S(1)}, u32[]{:S(2)}, u32[]{:S(2)}) collective-permute-start(f32[16,1024]{1,0:T(8,128)S(1)} %get-tuple-element.146.refs_0_), channel_id=1, source_target_pairs={{0,64},{8,72},{16,80},{24,88},{32,96},{40,104},{48,112},{56,120},{... | collective-permute-start | bytes 196616 | tf_op jit(solution)/shard_map/ppermute | solution.py:33
  75.4 21.9 %collective-permute-start.30 = (f32[16,1024]{1,0:T(8,128)S(1)}, f32[16,1024]{1,0:T(8,128)S(1)}, u32[]{:S(2)}, u32[]{:S(2)}) collective-permute-start(f32[16,1024]{1,0:T(8,128)S(1)} %get-tuple-element.146.refs_0_), channel_id=1, source_target_pairs={{0,128},{8,136},{16,144},{24,152},{32,160},{40,168},{48,176},{56,1... | collective-permute-start | bytes 196616 | tf_op jit(solution)/shard_map/ppermute | solution.py:33
  77.9 19.4 %collective-permute-start.31 = (f32[16,1024]{1,0:T(8,128)S(1)}, f32[16,1024]{1,0:T(8,128)S(1)}, u32[]{:S(2)}, u32[]{:S(2)}) collective-permute-start(f32[16,1024]{1,0:T(8,128)S(1)} %get-tuple-element.146.refs_0_), channel_id=1, source_target_pairs={{0,192},{8,200},{16,208},{24,216},{32,224},{40,232},{48,240},{56,2... | collective-permute-start | bytes 196616 | tf_op jit(solution)/shard_map/ppermute | solution.py:33
  98.6 21.4 %all-to-all-start.5 = ((f32[4,160,512]{2,1,0:T(8,128)}), f32[4,160,512]{2,1,0:T(8,128)S(1)}, u32[]{:S(2)}, u32[]{:S(2)}) async-start(f32[4,160,512]{2,1,0:T(8,128)} %tile.13), calls=%async_computation.5 | async-start | bytes 2621440 | tf_op jit(solution)/shard_map/all_to_all | solution.py:428
  103.0 16.2 %collective-permute-start.38 = (f32[32,1024]{1,0:T(8,128)S(1)}, f32[32,1024]{1,0:T(8,128)S(1)}, u32[]{:S(2)}, u32[]{:S(2)}) collective-permute-start(f32[32,1024]{1,0:T(8,128)S(1)} %get-tuple-element.163), channel_id=1, source_target_pairs={{0,64},{8,72},{16,80},{24,88},{32,96},{40,104},{48,112},{56,120},{... | collective-permute-start | bytes 393224 | tf_op jit(solution)/shard_map/ppermute | solution.py:38
  104.3 14.9 %collective-permute-start.39 = (f32[32,1024]{1,0:T(8,128)S(1)}, f32[32,1024]{1,0:T(8,128)S(1)}, u32[]{:S(2)}, u32[]{:S(2)}) collective-permute-start(f32[32,1024]{1,0:T(8,128)S(1)} %get-tuple-element.164), channel_id=1, source_target_pairs={{0,128},{8,136},{16,144},{24,152},{32,160},{40,168},{48,176},{56,1... | collective-permute-start | bytes 393224 | tf_op jit(solution)/shard_map/ppermute | solution.py:38
  105.6 13.6 %collective-permute-start.40 = (f32[32,1024]{1,0:T(8,128)}, f32[32,1024]{1,0:T(8,128)S(1)}, u32[]{:S(2)}, u32[]{:S(2)}) collective-permute-start(f32[32,1024]{1,0:T(8,128)} %get-tuple-element.165), channel_id=1, source_target_pairs={{0,192},{8,200},{16,208},{24,216},{32,224},{40,232},{48,240},{56,2... | collective-permute-start | bytes 393224 | tf_op jit(solution)/shard_map/ppermute | solution.py:38
  120.8 17.8 %all-to-all-start.7 = ((f32[8,32,256]{2,1,0:T(8,128)}), f32[8,32,256]{2,1,0:T(8,128)S(1)}, u32[]{:S(2)}, u32[]{:S(2)}) async-start(f32[8,32,256]{2,1,0:T(8,128)} %tile.15), calls=%async_computation.7 | async-start | bytes 524288 | tf_op jit(solution)/shard_map/all_to_all | solution.py:417
  128.2 26.1 %collective-permute-start.44 = (f32[64,1280]{1,0:T(8,128)S(1)}, f32[64,1280]{1,0:T(8,128)}, u32[]{:S(2)}, u32[]{:S(2)}) collective-permute-start(f32[64,1280]{1,0:T(8,128)S(1)} %get-tuple-element.169.refs_0_), channel_id=1, source_target_pairs={{0,8},{8,0},{16,24},{24,16},{32,40},{40,32},{48,56},{56,48},{64,72... | collective-permute-start | bytes 983048 | tf_op jit(solution)/shard_map/ppermute | solution.py:33
  136.4 17.8 %collective-permute-start.45 = (f32[64,1280]{1,0:T(8,128)}, f32[64,1280]{1,0:T(8,128)}, u32[]{:S(2)}, u32[]{:S(2)}) collective-permute-start(f32[64,1280]{1,0:T(8,128)} %collective-permute-done.41.refs_1_), channel_id=1, source_target_pairs={{0,8},{8,0},{16,24},{24,16},{32,40},{40,32},{48,56},{56,48},{64,72... | collective-permute-start | bytes 983048 | tf_op jit(solution)/shard_map/ppermute | solution.py:33
  136.4 17.8 %collective-permute-start.46 = (f32[64,1280]{1,0:T(8,128)}, f32[64,1280]{1,0:T(8,128)}, u32[]{:S(2)}, u32[]{:S(2)}) collective-permute-start(f32[64,1280]{1,0:T(8,128)} %collective-permute-done.42.refs_2_), channel_id=1, source_target_pairs={{0,8},{8,0},{16,24},{24,16},{32,40},{40,32},{48,56},{56,48},{64,72... | collective-permute-start | bytes 983048 | tf_op jit(solution)/shard_map/ppermute | solution.py:33
  138.5 15.7 %collective-permute-start.47 = (f32[64,1280]{1,0:T(8,128)}, f32[64,1280]{1,0:T(8,128)}, u32[]{:S(2)}, u32[]{:S(2)}) collective-permute-start(f32[64,1280]{1,0:T(8,128)} %collective-permute-done.43.refs_3_), channel_id=1, source_target_pairs={{0,8},{8,0},{16,24},{24,16},{32,40},{40,32},{48,56},{56,48},{64,72... | collective-permute-start | bytes 983048 | tf_op jit(solution)/shard_map/ppermute | solution.py:33
  138.6 15.9 %collective-permute-start.48 = (f32[32,1536]{1,0:T(8,128)S(1)}, f32[32,1536]{1,0:T(8,128)S(1)}, u32[]{:S(2)}, u32[]{:S(2)}) collective-permute-start(f32[32,1536]{1,0:T(8,128)S(1)} %pack_blocks.9.refs_8_), channel_id=1, source_target_pairs={{0,8},{8,0},{16,24},{24,16},{32,40},{40,32},{48,56},{56,48},{64,72... | collective-permute-start | bytes 589832 | tf_op jit(solution)/shard_map/ppermute | solution.py:33
  (24 other events, 273.1 us)
